TPU v7x, 512 devices: a whole 4x8x8 slice. The times are simulated.
512 devices in a mesh: leaf: 4 (over x), row: 16 (over z, core), col: 8 (over y).
Axes of the slice: x: 4, y: 8, z: 8, core: 2. Of those that a mesh axis runs over, the one named last changes fastest.
Arguments:
- widths: int32 [15], replicated, may hold values from 1024 to 2048, as said below
- bottom_lists: int32 [8, 32], P('leaf'), may hold values from 0 to 47, as said below
- root_inverse: bfloat16 [2048, 2048], P('row')
- second_panels: bfloat16 [4, 2048, 1024], P('leaf', 'row', 'col'), may hold values from -0.09375 to 0.09375
- second_inverse: bfloat16 [4, 1024, 2048], P('leaf', 'col', 'row')
- third_panels: bfloat16 [4, 2, 2048, 2048], P('leaf', None, 'row', 'col'), may hold values from -0.09375 to 0.09375
- third_inverse: bfloat16 [4, 2048, 2048], P('leaf', 'col', 'row')
- bottom_panels: bfloat16 [8, 4096, 2048], P('leaf', 'row', 'col'), may hold values from -0.09375 to 0.09375
- bottom_inverse: bfloat16 [8, 2048, 2048], P('leaf', 'col', 'row')
Outputs:
- second_off: bfloat16 [4, 2048, 1024], P('leaf', 'row', 'col')
- second_diag: bfloat16 [4, 1024, 2048], P('leaf', 'col', 'row')
- third_off: bfloat16 [4, 2, 2048, 2048], P('leaf', None, 'row', 'col')
- third_diag: bfloat16 [4, 2048, 2048], P('leaf', 'col', 'row')
- bottom_off: bfloat16 [8, 3, 2048, 2048], P('leaf', None, 'row', 'col')
- bottom_diag: bfloat16 [8, 2048, 2048], P('leaf', 'col', 'row')
Inputs may be any that keep to these rules, and one draw needn't show every extreme that they name: `widths`: some supernode has 2048 columns and some 2048/2. `bottom_lists`: row e lists 32 different blocks of 128 rows of its chain (root, then second-level ancestor, then parent, 16 blocks each) in increasing order; block 0 and all blocks of the parent are always listed.
All inputs are finite; a program needn't handle non-finite values.
Results may differ from a plain program's by a relative error of at most 0.015.
Values may be sent and summed in bfloat16 or wider, within the bound.
A program may use at most 64 MiB of HBM per device.

v0:
```python
import jax
import jax.numpy as jnp
from jax import lax
from jax.sharding import PartitionSpec as P

NODES = 15
BOTTOM = 8


def partner(block, axis, apart):
    count = lax.axis_size(axis)
    route = []
    for low in range(count):
        high = low | 1 << apart
        if high != low and high < count:
            route += [(low, high), (high, low)]
    return lax.ppermute(block, axis, route)


def node_width(widths, node_at):
    return jnp.sum(jnp.where(jnp.arange(widths.shape[0]) == node_at, widths, 0))


def chain_fold(flat_chain, tile_width, ancestors, shard_piece):
    piece_rows = shard_piece.shape[1]
    picked = jnp.concatenate(
        [
            lax.dynamic_slice_in_dim(flat_chain, level_at * tile_width, piece_rows, 1)
            for level_at in range(ancestors)
        ],
        axis=1,
    )
    stacked = shard_piece.reshape(ancestors * piece_rows, shard_piece.shape[2])
    return jnp.dot(picked, stacked, preferred_element_type=jnp.float32)


def local(
    widths,
    bottom_lists,
    root_inverse,
    second_panels,
    second_inverse,
    third_panels,
    third_inverse,
    bottom_panels,
    bottom_inverse,
):
    group_at = lax.axis_index("leaf")
    row_at = lax.axis_index("row")
    col_at = lax.axis_index("col")
    rows_dev = root_inverse.shape[0]
    tile_width = root_inverse.shape[1]
    half_cols = second_panels.shape[2]
    own_cols = third_panels.shape[3]
    half_at = group_at % 2
    parent_one = 1 + group_at // 2
    node_two = 3 + group_at
    row_first = row_at * rows_dev
    row_index = row_first + jnp.arange(rows_dev)
    root_width = node_width(widths, 0)
    root_mask = (row_index < root_width)[:, None] & (jnp.arange(tile_width) < root_width)[None, :]
    root_block = jnp.where(root_mask, root_inverse, 0)
    width_one = node_width(widths, parent_one)
    mask_rows_one = row_index < width_one
    first_col = half_at * (tile_width // 2) + col_at * half_cols
    mask_cols_one = first_col + jnp.arange(half_cols) < width_one
    panel_one = jnp.where(mask_cols_one[None, :], second_panels[0], 0)
    flat_piece = lax.all_gather(panel_one, "row", axis=0, tiled=True)
    product_one = jnp.dot(root_block, flat_piece, preferred_element_type=jnp.float32)
    off_one = (-product_one).astype(jnp.bfloat16)
    mine_half = lax.all_gather(off_one, "col", axis=1, tiled=True)
    other_half = partner(mine_half, "leaf", 0)
    off_full = jnp.where(
        half_at == 0,
        jnp.concatenate([mine_half, other_half], 1),
        jnp.concatenate([other_half, mine_half], 1),
    )
    term_one = lax.dot_general(
        panel_one, off_full, (((0,), (0,)), ((), ())), preferred_element_type=jnp.float32
    )
    summed_one = lax.psum_scatter(
        term_one.astype(jnp.bfloat16), "row", scatter_dimension=1, tiled=True
    ).astype(jnp.float32)
    inverse_one = jnp.where(
        mask_cols_one[:, None] & mask_rows_one[None, :], second_inverse[0], 0
    ).astype(jnp.float32)
    diag_one = (inverse_one - summed_one).astype(jnp.bfloat16)
    mine_diag = lax.all_gather(diag_one.T, "col", axis=1, tiled=True)
    other_diag = partner(mine_diag, "leaf", 0)
    diag_full = jnp.where(
        half_at == 0,
        jnp.concatenate([mine_diag, other_diag], 1),
        jnp.concatenate([other_diag, mine_diag], 1),
    )
    second_off = off_one[None]
    second_diag = diag_one[None]
    turned_one = lax.all_to_all(off_full, "row", split_axis=1, concat_axis=0, tiled=True)
    chain_two = jnp.stack(
        [jnp.concatenate([root_block, off_full], 1), jnp.concatenate([turned_one.T, diag_full], 1)],
        0,
    )
    flat_two = chain_two.reshape(2 * rows_dev, 2 * tile_width)
    first_own = col_at * own_cols
    width_two = node_width(widths, node_two)
    mask_cols_two = first_own + jnp.arange(own_cols) < width_two
    panel_two = jnp.where(mask_cols_two[None, None, :], third_panels[0], 0)
    product_two = chain_fold(
        flat_two, tile_width, 2, lax.all_gather(panel_two, "row", axis=1, tiled=True)
    )
    off_two = (-product_two).astype(jnp.bfloat16).reshape(2, rows_dev, own_cols)
    full_two = lax.all_gather(off_two, "col", axis=2, tiled=True)
    term_two = jnp.einsum("kin,kim->nm", panel_two, full_two, preferred_element_type=jnp.float32)
    summed_two = lax.psum_scatter(
        term_two.astype(jnp.bfloat16), "row", scatter_dimension=1, tiled=True
    ).astype(jnp.float32)
    mask_rows_two = row_index < width_two
    inverse_two = jnp.where(
        mask_cols_two[:, None] & mask_rows_two[None, :], third_inverse[0], 0
    ).astype(jnp.float32)
    diag_two = (inverse_two - summed_two).astype(jnp.bfloat16)
    diag_rows_two = lax.all_gather(diag_two.T, "col", axis=1, tiled=True)
    turned_two = lax.all_to_all(full_two, "row", split_axis=2, concat_axis=1, tiled=True)
    lower_two = jnp.transpose(turned_two, (2, 0, 1)).reshape(rows_dev, 2 * tile_width)
    chain_three = jnp.stack(
        [
            jnp.concatenate([chain_two[0], full_two[0]], 1),
            jnp.concatenate([chain_two[1], full_two[1]], 1),
            jnp.concatenate([lower_two, diag_rows_two], 1),
        ],
        0,
    )
    flat_three = chain_three.reshape(3 * rows_dev, 3 * tile_width)
    bottom_dev = bottom_panels.shape[0]
    list_len = bottom_lists.shape[1]
    block_rows = 2 * tile_width // list_len
    node_three = NODES - BOTTOM + bottom_dev * group_at + jnp.arange(bottom_dev)
    width_three = jnp.sum(
        jnp.where(jnp.arange(widths.shape[0])[None, :] == node_three[:, None], widths[None, :], 0),
        1,
    )
    mask_cols_three = (first_own + jnp.arange(own_cols))[None, :] < width_three[:, None]
    panel_three = jnp.where(mask_cols_three[:, None, :], bottom_panels, 0)
    positions = (
        jnp.repeat(bottom_lists, block_rows, axis=1) * block_rows
        + jnp.arange(list_len * block_rows) % block_rows
    )
    own_chain = (jnp.arange(3)[:, None] * tile_width + row_index[None, :]).reshape(-1)
    matches = bottom_lists[:, :, None] == (own_chain // block_rows)[None, None, :]
    member = jnp.any(matches, axis=1)
    lower_all = lax.all_gather(panel_three, "row", axis=1, tiled=True)
    spread = jax.vmap(
        lambda where_to, values_in: jnp.zeros((3 * tile_width, own_cols), jnp.bfloat16)
        .at[where_to]
        .set(values_in)
    )(positions, lower_all)
    product_three = jnp.einsum(
        "ab,ebn->ean", flat_three, spread, preferred_element_type=jnp.float32
    )
    chain_rows = lax.dynamic_slice_in_dim(
        spread.reshape(bottom_dev, 3, tile_width, own_cols), row_first, rows_dev, 2
    )
    off_three = jnp.where(member[:, :, None], -product_three, 0.0).astype(jnp.bfloat16)
    off_three = off_three.reshape(bottom_dev, 3, rows_dev, own_cols)
    full_three = lax.all_gather(off_three, "col", axis=3, tiled=True)
    term_three = jnp.einsum(
        "ekin,ekim->enm", chain_rows, full_three, preferred_element_type=jnp.float32
    )
    summed_three = lax.psum_scatter(
        term_three.astype(jnp.bfloat16), "row", scatter_dimension=2, tiled=True
    ).astype(jnp.float32)
    mask_rows_three = row_index[None, :] < width_three[:, None]
    inverse_three = jnp.where(
        mask_cols_three[:, :, None] & mask_rows_three[:, None, :], bottom_inverse, 0
    ).astype(jnp.float32)
    diag_three = (inverse_three - summed_three).astype(jnp.bfloat16)
    return (second_off, second_diag, off_two[None], diag_two[None], off_three, diag_three)


def solution(mesh):
    in_specs = (
        P(),
        P("leaf", None),
        P("row", None),
        P("leaf", "row", "col"),
        P("leaf", "col", "row"),
        P("leaf", None, "row", "col"),
        P("leaf", "col", "row"),
        P("leaf", "row", "col"),
        P("leaf", "col", "row"),
    )
    out_specs = (
        P("leaf", "row", "col"),
        P("leaf", "col", "row"),
        P("leaf", None, "row", "col"),
        P("leaf", "col", "row"),
        P("leaf", None, "row", "col"),
        P("leaf", "col", "row"),
    )
    return jax.shard_map(local, mesh=mesh, in_specs=in_specs, out_specs=out_specs, check_vma=False)
```

profile of v0, /device:TPU:8, one launch (start us, length us, event | category | flops | bytes accessed | tf_op | source)
XLA Modules:
  0.0 519.0 jit_solution(5305973732029650270)
XLA Ops:
  7.2 0.9 copy.58
  8.1 1.3 fusion.20
  10.2 24.6 %all_gather.24 = bf16[2048,128]{0,1:T(8,128)(2,1)S(1)} all-gather(bf16[128,128]{0,1:T(8,128)(2,1)S(1)} %bitcast_select_fusion.1), channel_id=1, replica_groups=mesh['leaf'=4,'row'=16,'col'=8] {'row'}, dimensions={0}, use_global_device_ids=true | all-gather | bytes 557056 | tf_op jit(solution)/shard_map/all_gather | solution.py:68
  35.5 0.7 broadcast_compare_fusion.5
  36.1 1.3 and_select_fusion
  37.7 23.5 %all_gather.25 = bf16[128,1024]{1,0:T(8,128)(2,1)S(1)} all-gather(bf16[128,128]{1,0:T(8,128)(2,1)S(1)} %fusion.7), channel_id=1, replica_groups=mesh['leaf'=4,'row'=16,'col'=8] {'col'}, dimensions={1}, use_global_device_ids=true | all-gather | bytes 294912 | tf_op jit(solution)/shard_map/all_gather | solution.py:71
  61.3 3.5 collective-permute-start
  64.8 4.9 collective-permute-done
  69.8 1.2 convolution_convert_fusion
  71.0 0.7 broadcast_compare_fusion.2
  71.7 0.7 bitcast_select_fusion
  72.5 0.9 maximum_select_fusion.1
  73.4 3.6 all-to-all-start
  77.1 0.7 broadcast_compare_fusion.4
  77.8 49.9 %reduce-scatter.6.cloned.1.call-done = bf16[128,128]{0,1:T(8,128)(2,1)} async-done(((bf16[128,2048]{0,1:T(8,128)(2,1)}), bf16[128,128]{0,1:T(8,128)(2,1)}) %reduce-scatter.6.cloned.1.call-update) | async-done | bytes 32784 | tf_op jit(solution)/shard_map/reduce_scatter | solution.py:81
  127.7 0.8 fusion.22
  128.6 23.1 %all_gather.26 = bf16[128,1024]{1,0:T(8,128)(2,1)S(1)} all-gather(bf16[128,128]{1,0:T(8,128)(2,1)S(1)} %get-tuple-element.37), channel_id=1, replica_groups=mesh['leaf'=4,'row'=16,'col'=8] {'col'}, dimensions={1}, use_global_device_ids=true | all-gather | bytes 294912 | tf_op jit(solution)/shard_map/all_gather | solution.py:88
  151.7 3.2 collective-permute-start.1
  155.2 4.8 collective-permute-done.1
  160.0 1.2 maximum_select_fusion.2
  161.3 1.5 pad_maximum_fusion.1
  162.8 9.9 %all-gather.5.cloned.1.call-done = bf16[2,2048,256]{2,1,0:T(8,128)(2,1)} async-done(((bf16[2,128,256]{2,1,0:T(8,128)(2,1)}), bf16[2,2048,256]{2,1,0:T(8,128)(2,1)}) %all-gather.5.cloned.1.call-update) | async-done | bytes 2097168 | tf_op jit(solution)/shard_map/all_gather | solution.py:108
  172.8 3.6 fusion.6
  176.5 39.9 %all-gather.7.cloned.1.call-done = bf16[2,128,2048]{2,1,0:T(8,128)(2,1)} async-done(((bf16[2,128,256]{2,1,0:T(8,128)(2,1)}), bf16[2,128,2048]{2,1,0:T(8,128)(2,1)}) %all-gather.7.cloned.1.call-update) | async-done | bytes 1048592 | tf_op jit(solution)/shard_map/all_gather | solution.py:111
  216.4 2.8 fusion.2
  219.6 0.7 broadcast_select_fusion
  220.8 2.0 copy.69
  222.8 7.5 %all-to-all-start.1 = ((bf16[2,128,2048]{1,0,2:T(2,128)(2,1)}), bf16[2,128,2048]{1,0,2:T(2,128)(2,1)}, u32[]{:S(2)}, u32[]{:S(2)}) async-start(bf16[2,128,2048]{1,0,2:T(2,128)(2,1)} %copy.69), calls=%async_computation.3 | async-start | bytes 2097152 | tf_op jit(solution)/shard_map/all_to_all | solution.py:122
  231.5 2.3 maximum_bitcast_fusion
  233.8 24.9 %all-to-all-done.1 = bf16[2,128,2048]{1,0,2:T(2,128)(2,1)} async-done(((bf16[2,128,2048]{1,0,2:T(2,128)(2,1)}), bf16[2,128,2048]{1,0,2:T(2,128)(2,1)}, u32[]{:S(2)}, u32[]{:S(2)}) %all-to-all-start.1) | async-done | bytes 1048608 | tf_op jit(solution)/shard_map/all_to_all | solution.py:122
  258.8 1.9 copy.95
  261.1 25.3 %reduce-scatter.8.cloned.1.call-done = bf16[256,128]{0,1:T(8,128)(2,1)} async-done(((bf16[256,2048]{0,1:T(8,128)(2,1)}), bf16[256,128]{0,1:T(8,128)(2,1)}) %reduce-scatter.8.cloned.1.call-update) | async-done | bytes 65552 | tf_op jit(solution)/shard_map/reduce_scatter | solution.py:113
  286.4 0.9 fusion.24
  287.3 25.9 %all_gather.30 = bf16[128,2048]{1,0:T(8,128)(2,1)S(1)} all-gather(bf16[128,256]{1,0:T(8,128)(2,1)S(1)} %get-tuple-element.35), channel_id=1, replica_groups=mesh['leaf'=4,'row'=16,'col'=8] {'col'}, dimensions={1}, use_global_device_ids=true | all-gather | bytes 589824 | tf_op jit(solution)/shard_map/all_gather | solution.py:121
  313.3 3.6 pad_maximum_fusion
  317.0 18.1 %all-gather.9.cloned.1.call-done = bf16[2,4096,256]{2,1,0:T(8,128)(2,1)} async-done(((bf16[2,256,256]{2,1,0:T(8,128)(2,1)}), bf16[2,4096,256]{2,1,0:T(8,128)(2,1)}) %all-gather.9.cloned.1.call-update) | async-done | bytes 4194320 | tf_op jit(solution)/shard_map/all_gather | solution.py:150
  335.1 39.1 %scatter_custom_fusion = bf16[12288,256]{1,0:T(8,128)(2,1)} fusion(s32[8192]{0:T(1024)S(1)} %bitcast.140, bf16[8192,256]{1,0:T(8,128)(2,1)} %bitcast.141, bf16[]{:T(256)} %constant.73.clone.1), kind=kCustom, calls=%fused_computation.3 | custom fusion | bytes 6291968
  374.1 7.6 %fusion.5 = bf16[2,384,256]{1,2,0:T(8,128)(2,1)S(1)} fusion(bf16[2,6144,256]{2,1,0:T(8,128)(2,1)} %bitcast.125, bf16[384,6144,1]{1,0,2:T(8,128)(2,1)} %bitcast.127, pred[2,384]{1,0:T(4,128)(4,1)S(1)} %compare_reduce_fusion), kind=kOutput, calls=%fused_computation.15 | convolution fusion | flops 2416508928 | bytes 11404032 | tf_op jit(solution)/shard_map/ab,ebn->ean/dot_general | solution.py:156
  381.7 0.9 copy.72
  382.7 57.5 %all-gather.11.cloned.1.call-done = bf16[2,3,128,2048]{3,2,1,0:T(8,128)(2,1)} async-done(((bf16[2,3,128,256]{3,2,1,0:T(8,128)(2,1)}), bf16[2,3,128,2048]{3,2,1,0:T(8,128)(2,1)}) %all-gather.11.cloned.1.call-update) | async-done | bytes 3145744 | tf_op jit(solution)/shard_map/all_gather | solution.py:164
  440.2 3.3 bitcast_convert_fusion
  443.6 3.8 copy.83
  447.4 3.4 copy.91
  450.9 0.7 copy.74
  451.6 0.7 copy.75
  452.3 57.9 %reduce-scatter.10.cloned.1.call-done = bf16[128,512]{1,0:T(8,128)(2,1)} async-done(((bf16[2048,512]{1,0:T(8,128)(2,1)}), bf16[128,512]{1,0:T(8,128)(2,1)}) %reduce-scatter.10.cloned.1.call-update) | async-done | bytes 131088
  510.3 0.9 reshape.268
  511.4 0.8 subtract_convert_fusion
  (77 shorter events, 5.3 us)
Async XLA Ops:
  7.2 64.5 %copy-start.5 = (bf16[1,2,128,256]{3,2,1,0:T(8,128)(2,1)S(1)}, bf16[1,2,128,256]{3,2,1,0:T(8,128)(2,1)}, u32[]{:S(2)}) copy-start(bf16[1,2,128,256]{3,2,1,0:T(8,128)(2,1)} %param.14) | copy-start | bytes 393220
  7.2 120.6 %reduce-scatter.6.cloned.1.call-start = ((), (), s32[]{:S(2)}) async-start(), calls=%async_computation.5 | async-start | bytes 557056 | tf_op jit(solution)/shard_map/reduce_scatter | solution.py:81
  37.7 35.7 %copy-start.4 = (bf16[128,128]{1,0:T(8,128)(2,1)}, bf16[128,128]{1,0:T(8,128)(2,1)S(1)}, u32[]{:S(2)}) copy-start(bf16[128,128]{1,0:T(8,128)(2,1)S(1)} %fusion.7) | copy-start | bytes 98308
  61.3 15.8 %copy-start.8 = (bf16[1,128,128]{2,1,0:T(8,128)(2,1)S(1)}, bf16[1,128,128]{2,1,0:T(8,128)(2,1)}, u32[]{:S(2)}) copy-start(bf16[1,128,128]{2,1,0:T(8,128)(2,1)} %param.13) | copy-start | bytes 98308
  61.3 8.4 %collective-permute-start = (bf16[128,1024]{1,0:T(8,128)(2,1)S(1)}, bf16[128,1024]{1,0:T(8,128)(2,1)S(1)}, u32[]{:S(2)}, u32[]{:S(2)}) collective-permute-start(bf16[128,1024]{1,0:T(8,128)(2,1)S(1)} %all_gather.25), channel_id=1, source_target_pairs={{0,128},{128,0},{256,384},{384,256},{1,129},{129,1},{257,385},{385... | collective-permute-start | bytes 786440 | tf_op jit(solution)/shard_map/ppermute | solution.py:17
  71.0 101.8 %all-gather.5.cloned.1.call-start = ((), (), s32[]{:S(2)}) async-start(), calls=%async_computation.6 | async-start | bytes 2228224 | tf_op jit(solution)/shard_map/all_gather | solution.py:108
  73.4 81.6 %all-to-all-start = ((bf16[128,16,128]{2,0,1:T(8,128)(2,1)}), bf16[128,16,128]{2,0,1:T(8,128)(2,1)S(1)}, u32[]{:S(2)}, u32[]{:S(2)}) async-start(bf16[128,16,128]{2,0,1:T(8,128)(2,1)} %maximum_select_fusion.1), calls=%async_computation.1 | async-start | bytes 1048576 | tf_op jit(solution)/shard_map/all_to_all | solution.py:97
  77.0 139.4 %all-gather.7.cloned.1.call-start = ((), (), s32[]{:S(2)}) async-start(), calls=%async_computation.7 | async-start | bytes 1179648 | tf_op jit(solution)/shard_map/all_gather | solution.py:111
  151.7 8.4 %collective-permute-start.1 = (bf16[128,1024]{1,0:T(8,128)(2,1)S(1)}, bf16[128,1024]{1,0:T(8,128)(2,1)}, u32[]{:S(2)}, u32[]{:S(2)}) collective-permute-start(bf16[128,1024]{1,0:T(8,128)(2,1)S(1)} %all_gather.26), channel_id=1, source_target_pairs={{0,128},{128,0},{256,384},{384,256},{1,129},{129,1},{257,385},{385... | collective-permute-start | bytes 786440 | tf_op jit(solution)/shard_map/ppermute | solution.py:17
  161.2 1.6 copy-start.1
  162.8 53.6 %copy-start.2 = (bf16[2,128,256]{2,1,0:T(8,128)(2,1)S(1)}, bf16[2,128,256]{2,1,0:T(8,128)(2,1)}, u32[]{:S(2)}) copy-start(bf16[2,128,256]{2,1,0:T(8,128)(2,1)} %bitcast_select_fusion) | copy-start | bytes 393220
  172.8 46.6 %copy-start.12 = (s32[15]{0:T(128)S(1)}, s32[15]{0:T(128)}, u32[]{:S(2)}) copy-start(s32[15]{0:T(128)} %param.9) | copy-start | bytes 184
  172.8 46.9 %copy-start.3 = (bf16[2,256,256]{2,1,0:T(8,128)(2,1)S(1)}, bf16[2,256,256]{2,1,0:T(8,128)(2,1)}, u32[]{:S(2)}) copy-start(bf16[2,256,256]{2,1,0:T(8,128)(2,1)} %param.16) | copy-start | bytes 786436
  176.4 44.0 %copy-start.9 = (s32[2,32]{1,0:T(2,128)S(1)}, s32[2,32]{1,0:T(2,128)}, u32[]{:S(2)}) copy-start(s32[2,32]{1,0:T(2,128)} %param.10) | copy-start | bytes 772
  176.4 44.2 %copy-start.11 = (s32[2]{0:T(128)S(1)}, s32[2]{0:T(128)}, u32[]{:S(2)}) copy-start(s32[2]{0:T(128)} %constant.94) | copy-start | bytes 28
  176.4 44.3 %copy-start.10 = (s32[2]{0:T(128)S(1)}, s32[2]{0:T(128)}, u32[]{:S(2)}) copy-start(s32[2]{0:T(128)} %constant.97) | copy-start | bytes 28
  176.4 110.0 %reduce-scatter.8.cloned.1.call-start = ((), (), s32[]{:S(2)}) async-start(), calls=%async_computation.8 | async-start | bytes 1114112 | tf_op jit(solution)/shard_map/reduce_scatter | solution.py:113
  216.4 4.4 copy-start
  219.2 11.2 %copy-start.7 = (bf16[1,256,128]{2,1,0:T(8,128)(2,1)S(1)}, bf16[1,256,128]{2,1,0:T(8,128)(2,1)}, u32[]{:S(2)}) copy-start(bf16[1,256,128]{2,1,0:T(8,128)(2,1)} %param.15) | copy-start | bytes 196612
  219.3 115.8 %all-gather.9.cloned.1.call-start = ((), (), s32[]{:S(2)}) async-start(), calls=%async_computation.9 | async-start | bytes 4456448 | tf_op jit(solution)/shard_map/all_gather | solution.py:150
  222.8 35.9 %all-to-all-start.1 = ((bf16[2,128,2048]{1,0,2:T(2,128)(2,1)}), bf16[2,128,2048]{1,0,2:T(2,128)(2,1)}, u32[]{:S(2)}, u32[]{:S(2)}) async-start(bf16[2,128,2048]{1,0,2:T(2,128)(2,1)} %copy.69), calls=%async_computation.3 | async-start | bytes 2097152 | tf_op jit(solution)/shard_map/all_to_all | solution.py:122
  230.4 209.9 %all-gather.11.cloned.1.call-start = ((), (), s32[]{:S(2)}) async-start(), calls=%async_computation.10 | async-start | bytes 3538944 | tf_op jit(solution)/shard_map/all_gather | solution.py:164
  382.7 127.6 %reduce-scatter.10.cloned.1.call-start = ((), (), s32[]{:S(2)}) async-start(), calls=%async_computation.11 | async-start | bytes 2228224
  447.4 64.0 %copy-start.6 = (bf16[2,256,128]{2,1,0:T(8,128)(2,1)S(1)}, bf16[2,256,128]{2,1,0:T(8,128)(2,1)}, u32[]{:S(2)}) copy-start(bf16[2,256,128]{2,1,0:T(8,128)(2,1)} %param.17) | copy-start | bytes 393220
Sparse Core Ops, SparseCore 0:
  71.1 56.6 reduce-scatter.5
  130.7 42.0 all-gather.4
  176.5 39.8 all-gather.6
  219.4 66.9 reduce-scatter.7
  288.9 46.0 all-gather.8
  382.8 57.3 all-gather.10
  450.9 59.3 reduce-scatter.9
where the time goes:
time: 520 us; the launch traced here: 519 us
  waiting for transfers between devices  293 us (56%)
  blocking collectives  97.1 us (19%)
  local copies, waits for them, and re-layouts  55.7 us (11%)
  other arithmetic  21.3 us (4%)
  matrix products  18.9 us (4%)
  starting transfers between devices  18.1 us (3%)
  between operations  14.6 us (3%)
    unnamed x8, waiting for transfers between devices  58.1 us
    all_gather x1, waiting for transfers between devices, local(): full_three = lax.all_gather(off_three, 'col', axis=3, tiled=True)  57.5 us
    unnamed x39, local copies, waits for them, and re-layouts  50.3 us
    reduce_scatter x1, waiting for transfers between devices, local(): lax.psum_scatter(term_one.astype(jnp.bfloat16), 'row', scatter_dimension=...  49.9 us
    all_gather x1, waiting for transfers between devices, local(): full_two = lax.all_gather(off_two, 'col', axis=2, tiled=True)  39.9 us
    all_gather x1, blocking collectives, local(): diag_rows_two = lax.all_gather(diag_two.T, 'col', axis=1, tiled=True)  25.9 us
    reduce_scatter x1, waiting for transfers between devices, local(): lax.psum_scatter(term_two.astype(jnp.bfloat16), 'row', scatter_dimension=...  25.3 us
    all_to_all x1, waiting for transfers between devices, local(): lax.all_to_all(full_two, 'row', split_axis=2, concat_axis=1, tiled=True)  24.9 us
  transfers between devices with their start and end apart: 11, of which 10 were waited for; matrix products, arithmetic and copies ran while one was open for 4% of the time, Pallas kernels for 0%

commit v1 on v0

--- a/solution.py
+++ b/solution.py
@@ -5,6 +5,11 @@
 
 NODES = 15
 BOTTOM = 8
+
+
+def exchange_gather(x, mesh_axis, along):
+    sent = jnp.stack([x] * lax.axis_size(mesh_axis))
+    return jnp.concatenate(lax.all_to_all(sent, mesh_axis, 0, 0), axis=along)
 
 
 def partner(block, axis, apart):
@@ -161,7 +166,7 @@
     )
     off_three = jnp.where(member[:, :, None], -product_three, 0.0).astype(jnp.bfloat16)
     off_three = off_three.reshape(bottom_dev, 3, rows_dev, own_cols)
-    full_three = lax.all_gather(off_three, "col", axis=3, tiled=True)
+    full_three = exchange_gather(off_three, "col", 3)
     term_three = jnp.einsum(
         "ekin,ekim->enm", chain_rows, full_three, preferred_element_type=jnp.float32
     )

time: 520 us -> 542 us (1.042)
  the two profiles are of different devices: /device:TPU:8 before, /device:TPU:2 now
where the time goes in v1:
time: 542 us; the launch traced here: 541 us
  waiting for transfers between devices  305 us (56%)
  blocking collectives  99.4 us (18%)
  local copies, waits for them, and re-layouts  58.1 us (11%)
  starting transfers between devices  23 us (4%)
  other arithmetic  22.6 us (4%)
  matrix products  17.9 us (3%)
  between operations  14.6 us (3%)
    all_to_all x1, waiting for transfers between devices, exchange_gather(): return jnp.concatenate(lax.all_to_all(sent, mesh_axis, 0, 0), axis=along)  74.2 us
    unnamed x7, waiting for transfers between devices  54.6 us
    unnamed x45, local copies, waits for them, and re-layouts  51 us
    reduce_scatter x1, waiting for transfers between devices, local(): lax.psum_scatter(term_one.astype(jnp.bfloat16), 'row', scatter_dimension=...  48.9 us
    all_gather x1, waiting for transfers between devices, local(): full_two = lax.all_gather(off_two, 'col', axis=2, tiled=True)  39.9 us
    all_gather x1, blocking collectives, local(): diag_rows_two = lax.all_gather(diag_two.T, 'col', axis=1, tiled=True)  25.9 us
    reduce_scatter x1, waiting for transfers between devices, local(): lax.psum_scatter(term_two.astype(jnp.bfloat16), 'row', scatter_dimension=...  25.4 us
    all_to_all x1, waiting for transfers between devices, local(): lax.all_to_all(full_two, 'row', split_axis=2, concat_axis=1, tiled=True)  25 us
  transfers between devices with their start and end apart: 11, of which 10 were waited for; matrix products, arithmetic and copies ran while one was open for 4% of the time, Pallas kernels for 0%

profile of v1, /device:TPU:2, one launch (start us, length us, event | category | flops | bytes accessed | tf_op | source)
XLA Modules:
  0.0 540.5 jit_solution(8663510564523422827)
XLA Ops:
  7.2 0.9 copy.59
  8.1 1.3 fusion.20
  10.2 24.6 %all_gather.21 = bf16[2048,128]{0,1:T(8,128)(2,1)S(1)} all-gather(bf16[128,128]{0,1:T(8,128)(2,1)S(1)} %bitcast_select_fusion.1), channel_id=1, replica_groups=mesh['leaf'=4,'row'=16,'col'=8] {'row'}, dimensions={0}, use_global_device_ids=true | all-gather | bytes 557056 | tf_op jit(solution)/shard_map/all_gather | solution.py:73
  35.5 0.7 broadcast_compare_fusion.5
  36.1 1.3 and_select_fusion
  38.3 25.0 %all_gather.22 = bf16[128,1024]{1,0:T(8,128)(2,1)S(1)} all-gather(bf16[128,128]{1,0:T(8,128)(2,1)S(1)} %fusion.7), channel_id=1, replica_groups=mesh['leaf'=4,'row'=16,'col'=8] {'col'}, dimensions={1}, use_global_device_ids=true | all-gather | bytes 294912 | tf_op jit(solution)/shard_map/all_gather | solution.py:76
  63.3 2.6 collective-permute-start
  65.9 5.8 %collective-permute-done = bf16[128,1024]{1,0:T(8,128)(2,1)S(1)} collective-permute-done((bf16[128,1024]{1,0:T(8,128)(2,1)S(1)}, bf16[128,1024]{1,0:T(8,128)(2,1)S(1)}, u32[]{:S(2)}, u32[]{:S(2)}) %collective-permute-start) | collective-permute-done | bytes 262176 | tf_op jit(solution)/shard_map/ppermute | solution.py:22
  71.8 1.2 convolution_convert_fusion
  73.7 0.7 bitcast_select_fusion
  74.5 0.9 maximum_select_fusion.1
  75.4 3.6 all-to-all-start
  79.2 0.7 broadcast_compare_fusion.4
  79.9 48.9 %reduce-scatter.6.cloned.1.call-done = bf16[128,128]{0,1:T(8,128)(2,1)} async-done(((bf16[128,2048]{0,1:T(8,128)(2,1)}), bf16[128,128]{0,1:T(8,128)(2,1)}) %reduce-scatter.6.cloned.1.call-update) | async-done | bytes 32784 | tf_op jit(solution)/shard_map/reduce_scatter | solution.py:86
  128.8 1.5 fusion.22
  130.2 24.0 %all_gather.23 = bf16[128,1024]{1,0:T(8,128)(2,1)S(1)} all-gather(bf16[128,128]{1,0:T(8,128)(2,1)S(1)} %get-tuple-element.37), channel_id=1, replica_groups=mesh['leaf'=4,'row'=16,'col'=8] {'col'}, dimensions={1}, use_global_device_ids=true | all-gather | bytes 294912 | tf_op jit(solution)/shard_map/all_gather | solution.py:93
  154.2 2.3 collective-permute-start.1
  156.9 5.7 %collective-permute-done.1 = bf16[128,1024]{1,0:T(8,128)(2,1)} collective-permute-done((bf16[128,1024]{1,0:T(8,128)(2,1)S(1)}, bf16[128,1024]{1,0:T(8,128)(2,1)}, u32[]{:S(2)}, u32[]{:S(2)}) %collective-permute-start.1) | collective-permute-done | bytes 262176 | tf_op jit(solution)/shard_map/ppermute | solution.py:22
  162.6 1.2 maximum_select_fusion.2
  163.8 1.5 pad_maximum_fusion.1
  165.3 8.1 %all-gather.4.cloned.1.call-done = bf16[2,2048,256]{2,1,0:T(8,128)(2,1)} async-done(((bf16[2,128,256]{2,1,0:T(8,128)(2,1)}), bf16[2,2048,256]{2,1,0:T(8,128)(2,1)}) %all-gather.4.cloned.1.call-update) | async-done | bytes 2097168 | tf_op jit(solution)/shard_map/all_gather | solution.py:113
  173.4 3.6 fusion.6
  177.1 39.9 %all-gather.6.cloned.1.call-done = bf16[2,128,2048]{2,1,0:T(8,128)(2,1)} async-done(((bf16[2,128,256]{2,1,0:T(8,128)(2,1)}), bf16[2,128,2048]{2,1,0:T(8,128)(2,1)}) %all-gather.6.cloned.1.call-update) | async-done | bytes 1048592 | tf_op jit(solution)/shard_map/all_gather | solution.py:116
  217.1 2.9 fusion.2
  220.3 0.7 broadcast_select_fusion
  221.5 2.0 copy.70
  223.5 7.5 %all-to-all-start.1 = ((bf16[2,128,2048]{1,0,2:T(2,128)(2,1)}), bf16[2,128,2048]{1,0,2:T(2,128)(2,1)}, u32[]{:S(2)}, u32[]{:S(2)}) async-start(bf16[2,128,2048]{1,0,2:T(2,128)(2,1)} %copy.70), calls=%async_computation.3 | async-start | bytes 2097152 | tf_op jit(solution)/shard_map/all_to_all | solution.py:127
  232.2 2.3 maximum_bitcast_fusion
  234.5 25.0 %all-to-all-done.1 = bf16[2,128,2048]{1,0,2:T(2,128)(2,1)} async-done(((bf16[2,128,2048]{1,0,2:T(2,128)(2,1)}), bf16[2,128,2048]{1,0,2:T(2,128)(2,1)}, u32[]{:S(2)}, u32[]{:S(2)}) %all-to-all-start.1) | async-done | bytes 1048608 | tf_op jit(solution)/shard_map/all_to_all | solution.py:127
  259.4 1.9 copy.98
  261.8 25.4 %reduce-scatter.8.cloned.1.call-done = bf16[256,128]{0,1:T(8,128)(2,1)} async-done(((bf16[256,2048]{0,1:T(8,128)(2,1)}), bf16[256,128]{0,1:T(8,128)(2,1)}) %reduce-scatter.8.cloned.1.call-update) | async-done | bytes 65552 | tf_op jit(solution)/shard_map/reduce_scatter | solution.py:118
  287.1 1.6 fusion.24
  288.7 25.9 %all_gather.27 = bf16[128,2048]{1,0:T(8,128)(2,1)S(1)} all-gather(bf16[128,256]{1,0:T(8,128)(2,1)S(1)} %get-tuple-element.35), channel_id=1, replica_groups=mesh['leaf'=4,'row'=16,'col'=8] {'col'}, dimensions={1}, use_global_device_ids=true | all-gather | bytes 589824 | tf_op jit(solution)/shard_map/all_gather | solution.py:126
  314.7 3.6 pad_maximum_fusion
  318.3 17.4 %all-gather.8.cloned.1.call-done = bf16[2,4096,256]{2,1,0:T(8,128)(2,1)} async-done(((bf16[2,256,256]{2,1,0:T(8,128)(2,1)}), bf16[2,4096,256]{2,1,0:T(8,128)(2,1)}) %all-gather.8.cloned.1.call-update) | async-done | bytes 4194320 | tf_op jit(solution)/shard_map/all_gather | solution.py:155
  335.8 39.1 %scatter_custom_fusion = bf16[12288,256]{1,0:T(8,128)(2,1)} fusion(s32[8192]{0:T(1024)S(1)} %bitcast.145, bf16[8192,256]{1,0:T(8,128)(2,1)} %bitcast.146, bf16[]{:T(256)} %constant.73.clone.1), kind=kCustom, calls=%fused_computation.3 | custom fusion | bytes 6291968
  374.8 7.6 %fusion.5 = bf16[2,384,256]{1,2,0:T(8,128)(2,1)S(1)} fusion(bf16[2,6144,256]{2,1,0:T(8,128)(2,1)} %bitcast.130, bf16[384,6144,1]{1,0,2:T(8,128)(2,1)} %bitcast.132, pred[2,384]{1,0:T(4,128)(4,1)S(1)} %compare_reduce_fusion), kind=kOutput, calls=%fused_computation.15 | convolution fusion | flops 2416508928 | bytes 11404032 | tf_op jit(solution)/shard_map/ab,ebn->ean/dot_general | solution.py:161
  382.6 2.1 stack.31
  384.7 6.7 %all-to-all-start.2 = ((bf16[8,2,3,128,256]{4,3,2,1,0:T(8,128)(2,1)}), bf16[8,2,3,128,256]{4,3,2,1,0:T(8,128)(2,1)S(1)}, u32[]{:S(2)}, u32[]{:S(2)}) async-start(bf16[8,2,3,128,256]{4,3,2,1,0:T(8,128)(2,1)} %stack.31), calls=%async_computation.4 | async-start | bytes 6291456 | tf_op jit(solution)/shard_map/all_to_all | solution.py:12
  391.5 74.2 %all-to-all-done.2 = bf16[8,2,3,128,256]{4,3,2,1,0:T(8,128)(2,1)S(1)} async-done(((bf16[8,2,3,128,256]{4,3,2,1,0:T(8,128)(2,1)}), bf16[8,2,3,128,256]{4,3,2,1,0:T(8,128)(2,1)S(1)}, u32[]{:S(2)}, u32[]{:S(2)}) %all-to-all-start.2) | async-done | bytes 3145760 | tf_op jit(solution)/shard_map/all_to_all | solution.py:12
  466.1 2.3 bitcast_convert_fusion
  468.4 3.8 copy.85
  472.3 3.4 copy.94
  475.8 0.7 copy.76
  476.5 0.7 copy.77
  477.3 54.6 %reduce-scatter.10.cloned.1.call-done = bf16[128,512]{1,0:T(8,128)(2,1)} async-done(((bf16[2048,512]{1,0:T(8,128)(2,1)}), bf16[128,512]{1,0:T(8,128)(2,1)}) %reduce-scatter.10.cloned.1.call-update) | async-done | bytes 131088
  531.8 0.9 reshape.278
  532.9 0.8 subtract_convert_fusion
  (84 shorter events, 7.1 us)
Async XLA Ops:
  7.2 66.5 %copy-start.7 = (bf16[1,2,128,256]{3,2,1,0:T(8,128)(2,1)S(1)}, bf16[1,2,128,256]{3,2,1,0:T(8,128)(2,1)}, u32[]{:S(2)}) copy-start(bf16[1,2,128,256]{3,2,1,0:T(8,128)(2,1)} %param.14) | copy-start | bytes 393220
  7.2 121.6 %reduce-scatter.6.cloned.1.call-start = ((), (), s32[]{:S(2)}) async-start(), calls=%async_computation.6 | async-start | bytes 557056 | tf_op jit(solution)/shard_map/reduce_scatter | solution.py:86
  37.7 0.6 copy-start.6
  63.3 15.8 %copy-start.11 = (bf16[1,128,128]{2,1,0:T(8,128)(2,1)S(1)}, bf16[1,128,128]{2,1,0:T(8,128)(2,1)}, u32[]{:S(2)}) copy-start(bf16[1,128,128]{2,1,0:T(8,128)(2,1)} %param.13) | copy-start | bytes 98308
  63.3 8.4 %collective-permute-start = (bf16[128,1024]{1,0:T(8,128)(2,1)S(1)}, bf16[128,1024]{1,0:T(8,128)(2,1)S(1)}, u32[]{:S(2)}, u32[]{:S(2)}) collective-permute-start(bf16[128,1024]{1,0:T(8,128)(2,1)S(1)} %all_gather.22), channel_id=1, source_target_pairs={{0,128},{128,0},{256,384},{384,256},{1,129},{129,1},{257,385},{385... | collective-permute-start | bytes 786440 | tf_op jit(solution)/shard_map/ppermute | solution.py:22
  73.0 100.4 %all-gather.4.cloned.1.call-start = ((), (), s32[]{:S(2)}) async-start(), calls=%async_computation.7 | async-start | bytes 2228224 | tf_op jit(solution)/shard_map/all_gather | solution.py:113
  75.4 81.2 %all-to-all-start = ((bf16[128,16,128]{2,0,1:T(8,128)(2,1)}), bf16[128,16,128]{2,0,1:T(8,128)(2,1)S(1)}, u32[]{:S(2)}, u32[]{:S(2)}) async-start(bf16[128,16,128]{2,0,1:T(8,128)(2,1)} %maximum_select_fusion.1), calls=%async_computation.1 | async-start | bytes 1048576 | tf_op jit(solution)/shard_map/all_to_all | solution.py:102
  79.0 138.1 %all-gather.6.cloned.1.call-start = ((), (), s32[]{:S(2)}) async-start(), calls=%async_computation.8 | async-start | bytes 1179648 | tf_op jit(solution)/shard_map/all_gather | solution.py:116
  154.2 8.4 %collective-permute-start.1 = (bf16[128,1024]{1,0:T(8,128)(2,1)S(1)}, bf16[128,1024]{1,0:T(8,128)(2,1)}, u32[]{:S(2)}, u32[]{:S(2)}) collective-permute-start(bf16[128,1024]{1,0:T(8,128)(2,1)S(1)} %all_gather.23), channel_id=1, source_target_pairs={{0,128},{128,0},{256,384},{384,256},{1,129},{129,1},{257,385},{385... | collective-permute-start | bytes 786440 | tf_op jit(solution)/shard_map/ppermute | solution.py:22
  163.8 1.6 copy-start.1
  165.3 51.7 %copy-start.3 = (bf16[2,128,256]{2,1,0:T(8,128)(2,1)S(1)}, bf16[2,128,256]{2,1,0:T(8,128)(2,1)}, u32[]{:S(2)}) copy-start(bf16[2,128,256]{2,1,0:T(8,128)(2,1)} %bitcast_select_fusion) | copy-start | bytes 393220
  173.4 46.6 %copy-start.15 = (s32[15]{0:T(128)S(1)}, s32[15]{0:T(128)}, u32[]{:S(2)}) copy-start(s32[15]{0:T(128)} %param.9) | copy-start | bytes 184
  173.4 46.9 %copy-start.4 = (bf16[2,256,256]{2,1,0:T(8,128)(2,1)S(1)}, bf16[2,256,256]{2,1,0:T(8,128)(2,1)}, u32[]{:S(2)}) copy-start(bf16[2,256,256]{2,1,0:T(8,128)(2,1)} %param.16) | copy-start | bytes 786436
  177.1 44.0 %copy-start.12 = (s32[2,32]{1,0:T(2,128)S(1)}, s32[2,32]{1,0:T(2,128)}, u32[]{:S(2)}) copy-start(s32[2,32]{1,0:T(2,128)} %param.10) | copy-start | bytes 772
  177.1 44.2 %copy-start.14 = (s32[2]{0:T(128)S(1)}, s32[2]{0:T(128)}, u32[]{:S(2)}) copy-start(s32[2]{0:T(128)} %constant.94) | copy-start | bytes 28
  177.1 44.3 %copy-start.13 = (s32[2]{0:T(128)S(1)}, s32[2]{0:T(128)}, u32[]{:S(2)}) copy-start(s32[2]{0:T(128)} %constant.97) | copy-start | bytes 28
  177.1 110.0 %reduce-scatter.8.cloned.1.call-start = ((), (), s32[]{:S(2)}) async-start(), calls=%async_computation.9 | async-start | bytes 1114112 | tf_op jit(solution)/shard_map/reduce_scatter | solution.py:118
  217.1 4.4 copy-start
  219.9 11.2 %copy-start.10 = (bf16[1,256,128]{2,1,0:T(8,128)(2,1)S(1)}, bf16[1,256,128]{2,1,0:T(8,128)(2,1)}, u32[]{:S(2)}) copy-start(bf16[1,256,128]{2,1,0:T(8,128)(2,1)} %param.15) | copy-start | bytes 196612
  220.0 115.8 %all-gather.8.cloned.1.call-start = ((), (), s32[]{:S(2)}) async-start(), calls=%async_computation.10 | async-start | bytes 4456448 | tf_op jit(solution)/shard_map/all_gather | solution.py:155
  223.5 35.9 %all-to-all-start.1 = ((bf16[2,128,2048]{1,0,2:T(2,128)(2,1)}), bf16[2,128,2048]{1,0,2:T(2,128)(2,1)}, u32[]{:S(2)}, u32[]{:S(2)}) async-start(bf16[2,128,2048]{1,0,2:T(2,128)(2,1)} %copy.70), calls=%async_computation.3 | async-start | bytes 2097152 | tf_op jit(solution)/shard_map/all_to_all | solution.py:127
  382.6 2.1 copy-start.2
  384.7 81.0 %all-to-all-start.2 = ((bf16[8,2,3,128,256]{4,3,2,1,0:T(8,128)(2,1)}), bf16[8,2,3,128,256]{4,3,2,1,0:T(8,128)(2,1)S(1)}, u32[]{:S(2)}, u32[]{:S(2)}) async-start(bf16[8,2,3,128,256]{4,3,2,1,0:T(8,128)(2,1)} %stack.31), calls=%async_computation.4 | async-start | bytes 6291456 | tf_op jit(solution)/shard_map/all_to_all | solution.py:12
  391.5 140.3 %reduce-scatter.10.cloned.1.call-start = ((), (), s32[]{:S(2)}) async-start(), calls=%async_computation.11 | async-start | bytes 2228224
  472.3 3.5 copy-start.9
  472.3 4.2 copy-start.5
  472.3 60.6 %copy-start.8 = (bf16[2,256,128]{2,1,0:T(8,128)(2,1)S(1)}, bf16[2,256,128]{2,1,0:T(8,128)(2,1)}, u32[]{:S(2)}) copy-start(bf16[2,256,128]{2,1,0:T(8,128)(2,1)} %param.17) | copy-start | bytes 393220
Sparse Core Ops, SparseCore 0:
  73.1 55.5 reduce-scatter.5
  131.7 41.6 all-gather.3
  177.2 39.8 all-gather.5
  220.1 67.0 reduce-scatter.7
  289.7 46.0 all-gather.7
  475.8 55.9 reduce-scatter.9
